TPU v7x, 32 devices: a whole 2x2x4 slice. The times are simulated.
32 devices in a mesh: req: 8 (over z, x), tp: 4 (over y, core).
Axes of the slice: x: 2, y: 2, z: 4, core: 2. Of those that a mesh axis runs over, the one named last changes fastest.
Arguments:
- x_pre: bfloat16 [4096, 1280], P('req', 'tp'), may hold values from -6 to 6
- x_dec: bfloat16 [32, 1280], P('req', 'tp'), may hold values from -6 to 6
- norm_gain: float32 [1280], replicated, may hold values from 0.1 to 1.9
- w_qkv: bfloat16 [3, 1280, 1280], P(None, None, 'tp'), may hold values from -0.15625 to 0.15625
- w_out: bfloat16 [1280, 1280], P('tp'), may hold values from -0.625 to 0.625
- pre_keys: bfloat16 [3072, 1280], P('req', 'tp'), may hold values from -70 to 70
- pre_values: bfloat16 [3072, 1280], P('req', 'tp'), may hold values from -6 to 6
- pre_lens: int32 [8], P('req'), may hold values from 0 to 384, as said below
- dec_keys: bfloat16 [5120, 1280], P('req', 'tp'), may hold values from -70 to 70
- dec_values: bfloat16 [5120, 1280], P('req', 'tp'), may hold values from -6 to 6
- dec_lens: int32 [32], replicated, may hold values from 1 to 3200, as said below
Outputs:
- pre_out: bfloat16 [4096, 1280], P('req', 'tp')
- dec_out: bfloat16 [32, 1280], P('req', 'tp')
Inputs may be any that keep to these rules, and one draw needn't show every extreme that they name: `pre_lens`: at least one prefill block has all 384 cached rows valid. `dec_lens`: the lengths sum to 3840; request 0 has exactly 3200 rows, every other request fewer.
All inputs are finite; a program needn't handle non-finite values.
Results may differ from a plain program's by a relative error of at most 0.012.
The roundings to bfloat16 on the way count: a program that leaves them out, or rounds other values in their place, can miss the bound.
Values may be sent and summed in bfloat16 or wider, within the bound.
A program may use at most 64 MiB of HBM per device.

v0:
```python
import math

import jax
import jax.numpy as jnp
from jax import lax
from jax.sharding import PartitionSpec as P

HD = 80


EPSILON = 1e-06
MASKED_SCORE = -1e30


def normalize(tokens, norm_gain):
    tokens_f = tokens.astype(jnp.float32)
    mean_square = jnp.mean(tokens_f * tokens_f, axis=-1, keepdims=True)
    return (tokens_f * lax.rsqrt(mean_square + EPSILON) * norm_gain).astype(jnp.bfloat16)


def project(hidden, w_qkv):
    return tuple(
        (
            jnp.dot(hidden, w_qkv[matrix_index], preferred_element_type=jnp.float32).astype(
                jnp.bfloat16
            )
            for matrix_index in range(3)
        )
    )


def rounded(weights):
    held = lax.optimization_barrier(weights.astype(jnp.bfloat16))
    return held.astype(jnp.float32)


def prefill_attention(
    query_pre, key_pre, value_pre, pre_keys, pre_values, prefix, local_heads, score_scale
):
    rows_pre = query_pre.shape[0]
    cached = pre_keys.shape[0]
    keys_all = jnp.concatenate([pre_keys, key_pre], axis=0).reshape(-1, local_heads, HD)
    values_all = jnp.concatenate([pre_values, value_pre], axis=0).reshape(-1, local_heads, HD)
    scores = (
        jnp.einsum(
            "phd,rhd->hpr",
            query_pre.reshape(rows_pre, local_heads, HD),
            keys_all,
            preferred_element_type=jnp.float32,
        )
        * score_scale
    )
    column = jnp.arange(keys_all.shape[0], dtype=jnp.int32)[None, :]
    position = jnp.arange(rows_pre, dtype=jnp.int32)[:, None]
    allowed = jnp.where(column < cached, column < prefix, column - cached <= position)
    scores = jnp.where(allowed[None], scores, MASKED_SCORE)
    row_top = jnp.max(scores, axis=-1, keepdims=True)
    weights = jnp.where(allowed[None], jnp.exp(scores - row_top), 0.0)
    totals = jnp.transpose(jnp.sum(weights, axis=-1))
    mixed = (
        jnp.einsum(
            "hpr,rhd->phd",
            weights.astype(jnp.bfloat16),
            values_all,
            preferred_element_type=jnp.float32,
        )
        / totals[..., None]
    )
    return mixed.reshape(rows_pre, local_heads * HD).astype(jnp.bfloat16)


def body(
    x_pre,
    x_dec,
    norm_gain,
    w_qkv,
    w_out,
    pre_keys,
    pre_values,
    pre_lens,
    dec_keys,
    dec_values,
    dec_lens,
):
    full_pre, full_dec = (
        lax.all_gather(x_pre, "tp", axis=1, tiled=True),
        lax.all_gather(x_dec, "tp", axis=1, tiled=True),
    )
    local_width = w_qkv.shape[2]
    local_heads = local_width // HD
    score_scale = 1.0 / math.sqrt(HD)
    query_pre, key_pre, value_pre = project(normalize(full_pre, norm_gain), w_qkv)
    query_dec, key_dec, value_dec = project(normalize(full_dec, norm_gain), w_qkv)
    attn_pre = prefill_attention(
        query_pre, key_pre, value_pre, pre_keys, pre_values, pre_lens[0], local_heads, score_scale
    )
    all_queries = lax.all_gather(query_dec, "req", axis=0, tiled=True)
    requests = all_queries.shape[0]
    own_rows = query_dec.shape[0]
    pool_rows = dec_keys.shape[0]
    device = lax.axis_index("req")
    starts = jnp.cumsum(dec_lens) - dec_lens
    global_rows = device * pool_rows + jnp.arange(pool_rows, dtype=jnp.int32)
    allowed = (global_rows[None, :] >= starts[:, None]) & (
        global_rows[None, :] < (starts + dec_lens)[:, None]
    )
    cache_scores = (
        jnp.einsum(
            "qhd,rhd->qhr",
            all_queries.reshape(requests, local_heads, HD),
            dec_keys.reshape(pool_rows, local_heads, HD),
            preferred_element_type=jnp.float32,
        )
        * score_scale
    )
    cache_scores = jnp.where(allowed[:, None, :], cache_scores, MASKED_SCORE)
    self_score = (
        jnp.sum(
            query_dec.astype(jnp.float32).reshape(own_rows, local_heads, HD)
            * key_dec.astype(jnp.float32).reshape(own_rows, local_heads, HD),
            axis=-1,
        )
        * score_scale
    )
    self_rows = lax.dynamic_update_slice_in_dim(
        jnp.full((requests, local_heads), MASKED_SCORE, jnp.float32),
        self_score,
        device * own_rows,
        0,
    )
    local_top = jnp.maximum(jnp.max(cache_scores, axis=-1), self_rows)
    row_top = lax.pmax(local_top, "req")
    weights = jnp.where(allowed[:, None, :], jnp.exp(cache_scores - row_top[..., None]), 0.0)
    totals = jnp.sum(weights, axis=-1)
    partial_value = jnp.einsum(
        "qhr,rhd->qhd",
        weights.astype(jnp.bfloat16),
        dec_values.reshape(pool_rows, local_heads, HD),
        preferred_element_type=jnp.float32,
    ).reshape(requests, local_width)
    totals_all, partial_all = lax.psum((totals, partial_value), "req")
    own_totals = lax.dynamic_slice_in_dim(totals_all, device * own_rows, own_rows, 0)
    own_partial = lax.dynamic_slice_in_dim(partial_all, device * own_rows, own_rows, 0)
    own_top = lax.dynamic_slice_in_dim(row_top, device * own_rows, own_rows, 0)
    self_weight = jnp.exp(self_score - own_top)
    numerator = own_partial.reshape(own_rows, local_heads, HD) + rounded(self_weight)[
        ..., None
    ] * value_dec.astype(jnp.float32).reshape(own_rows, local_heads, HD)
    denominator = own_totals + self_weight
    attn_dec = (
        (numerator / denominator[..., None]).reshape(own_rows, local_width).astype(jnp.bfloat16)
    )
    terms_pre = jnp.dot(attn_pre, w_out, preferred_element_type=jnp.float32)
    terms_dec = jnp.dot(attn_dec, w_out, preferred_element_type=jnp.float32)
    out_pre, out_dec = (
        lax.psum_scatter(terms_pre, "tp", scatter_dimension=1, tiled=True),
        lax.psum_scatter(terms_dec, "tp", scatter_dimension=1, tiled=True),
    )
    return (out_pre.astype(jnp.bfloat16), out_dec.astype(jnp.bfloat16))


def solution(mesh):
    return jax.shard_map(
        body,
        mesh=mesh,
        in_specs=(
            P("req", "tp"),
            P("req", "tp"),
            P(),
            P(None, None, "tp"),
            P("tp", None),
            P("req", "tp"),
            P("req", "tp"),
            P("req"),
            P("req", "tp"),
            P("req", "tp"),
            P(),
        ),
        out_specs=(P("req", "tp"), P("req", "tp")),
        check_vma=False,
    )
```

profile of v0, /device:TPU:0, one launch (start us, length us, event | category | flops | bytes accessed | tf_op | source)
XLA Modules:
  0.0 178.0 jit_solution(5210827561188687188)
XLA Ops:
  7.2 0.7 all-gather.4.cloned.1.call-update
  8.0 6.3 %all-gather = bf16[4,320,4]{1,2,0:T(4,128)(2,1)S(1)} all-gather(bf16[1,320,4]{1,2,0:T(4,128)(2,1)} %bitcast.66), channel_id=1, replica_groups=mesh['req'=8,'tp'=4] {'tp'}, dimensions={0}, use_global_device_ids=true | all-gather | bytes 12800 | tf_op jit(solution)/shard_map/all_gather | solution.py:87
  14.4 0.1 multiply_reduce_fusion
  14.5 0.8 multiply_convert_fusion
  15.3 1.4 convolution_convert_fusion.5
  16.7 31.1 %all-gather.1 = bf16[8,4,320]{2,1,0:T(4,128)(2,1)S(1)} all-gather(bf16[1,4,320]{2,1,0:T(4,128)(2,1)S(1)} %bitcast.65), channel_id=1, replica_groups=mesh['req'=8,'tp'=4] {'req'}, dimensions={0}, use_global_device_ids=true | all-gather | bytes 23040 | tf_op jit(solution)/shard_map/all_gather | solution.py:97
  48.0 0.7 copy.32
  48.8 0.1 reduce.1
  48.9 0.7 sub.28
  49.5 1.4 fusion.30
  51.0 0.1 mul.96
  51.1 0.1 reduce_sum.48
  51.3 0.1 dynamic_update_slice.3
  51.5 0.3 fusion.62
  51.8 21.3 %pmax.7 = f32[32,4]{0,1:T(4,128)S(1)} all-reduce(f32[32,4]{0,1:T(4,128)S(1)} %max.5), channel_id=1, replica_groups=mesh['req'=8,'tp'=4] {'req'}, use_global_device_ids=true, to_apply=%region_8.9 | all-reduce | flops 128 | bytes 1024 | tf_op jit(solution)/shard_map/pmax | solution.py:132
  73.1 0.3 convolution_bitcast_fusion.1
  73.6 0.2 fusion.45
  73.8 33.5 %all-reduce = (f32[32,4]{0,1:T(4,128)S(1)}, f32[32,320]{1,0:T(8,128)S(1)}) all-reduce(f32[32,4]{0,1:T(4,128)S(1)} %fusion.45, f32[32,320]{1,0:T(8,128)S(1)} %reshape.203), channel_id=1, replica_groups=mesh['req'=8,'tp'=4] {'req'}, use_global_device_ids=true, to_apply=%region_11.12 | all-reduce | flops 10368 | bytes 82944 | tf_op jit(solution)/shard_map/psum | solution.py:141
  108.0 2.9 %convolution_bitcast_fusion = f32[1280,4]{1,0:T(8,128)} fusion(bf16[320,1280]{1,0:T(8,128)(2,1)S(1)} %copy-done, f32[4,320]{1,0:T(4,128)S(1)} %div.34, f32[4,320]{1,0:T(4,128)S(1)} %mul.100, bf16[1280,4]{0,1:T(4,128)(2,1)S(1)} %multiply_convert_fusion, bf16[3,1280,320]{1,2,0:T(8,128)(2,1)} %param.14, f32[32,320]{1,0:T(8,128)S(1)} %get-tuple-element.3, ...), kind=kOutput, calls=%fused_computation.15 | convolution fusion | flops 6561280 | bytes 1687556
  111.7 1.1 fusion.12
  112.8 1.7 fusion.9
  114.5 2.1 %convolution_convert_fusion.2 = bf16[512,320]{0,1:T(8,128)(2,1)S(1)} fusion(bf16[3,1280,320]{1,2,0:T(8,128)(2,1)S(1)} %copy-done.1, bf16[512,1280]{0,1:T(8,128)(2,1)} %all-gather.4.cloned.1.call-done, f32[1280]{0:T(1024)S(1)} %copy-done.8, f32[512]{0:T(512)S(1)} %add_rsqrt_fusion), kind=kOutput, calls=%fused_computation.23 | convolution fusion | flops 422215680 | bytes 2467840 | tf_op jit(solution)/shard_map/dot_general | solution.py:24
  116.7 0.9 pad_maximum_fusion
  117.5 0.7 convolution_convert_fusion
  118.2 0.9 pad_maximum_fusion.1
  119.1 1.4 convolution_convert_fusion.1
  120.5 6.7 %fusion.61 = (f32[4,512]{1,0:T(4,128)S(1)}, bf16[4,512,896]{2,1,0:T(8,128)(2,1)}) fusion(bf16[512,4,80]{0,2,1:T(8,128)(2,1)} %bitcast.68, bf16[896,4,80]{0,2,1:T(8,128)(2,1)} %bitcast.60, pred[512,896]{1,0:T(8,128)(4,1)} %fusion.12), kind=kOutput, calls=%fused_computation.77 | convolution fusion | flops 304612224 | bytes 5038080 | tf_op jit(solution)/shard_map/sub | solution.py:58
  127.2 3.3 %fusion.19 = bf16[512,4,80]{0,2,1:T(8,128)(2,1)S(1)} fusion(bf16[896,4,80]{0,2,1:T(8,128)(2,1)S(1)} %bitcast.59, bf16[4,512,896]{2,1,0:T(8,128)(2,1)} %get-tuple-element.7, f32[512,4]{0,1:T(4,128)S(1)} %bitcast.69), kind=kOutput, calls=%fused_computation.20 | convolution fusion | flops 293928960 | bytes 4579328 | tf_op jit(solution)/shard_map/hpr,rhd->phd/dot_general | solution.py:61
  130.5 2.4 %fusion.63 = f32[512,1280]{0,1:T(8,128)} fusion(bf16[512,320]{0,1:T(8,128)(2,1)S(1)} %bitcast.63, bf16[320,1280]{1,0:T(8,128)(2,1)S(1)} %copy-done), kind=kOutput, calls=%fused_computation.79 | convolution fusion | flops 419430400 | bytes 3768320 | tf_op jit(solution)/shard_map/dot_general | solution.py:153
  133.0 1.6 copy.40
  134.6 35.0 %reduce-scatter.5.cloned.1.call-done = f32[512,320]{0,1:T(8,128)} async-done(((f32[512,1280]{0,1:T(8,128)}), f32[512,320]{0,1:T(8,128)}) %reduce-scatter.5.cloned.1.call-update) | async-done | bytes 655376 | tf_op jit(solution)/shard_map/reduce_scatter | solution.py:156
  169.6 1.9 %convert_element_type.74 = bf16[512,320]{0,1:T(8,128)(2,1)} convert(f32[512,320]{0,1:T(8,128)} %reduce-scatter.5.cloned.1.call-done) | non-fusion elementwise | flops 163840 | bytes 983040 | tf_op jit(solution)/shard_map/convert_element_type | solution.py:159
  (48 shorter events, 1.4 us)
Async XLA Ops:
  7.2 100.8 %copy-start = (bf16[320,1280]{1,0:T(8,128)(2,1)S(1)}, bf16[320,1280]{1,0:T(8,128)(2,1)}, u32[]{:S(2)}) copy-start(bf16[320,1280]{1,0:T(8,128)(2,1)} %param.15) | copy-start | bytes 2457604
  7.2 44.4 %copy-start.4 = (bf16[640,320]{0,1:T(8,128)(2,1)S(1)}, bf16[640,320]{0,1:T(8,128)(2,1)}, u32[]{:S(2)}) copy-start(bf16[640,320]{0,1:T(8,128)(2,1)} %param.19) | copy-start | bytes 1228804
  7.2 66.0 %copy-start.5 = (bf16[640,320]{0,1:T(8,128)(2,1)S(1)}, bf16[640,320]{0,1:T(8,128)(2,1)}, u32[]{:S(2)}) copy-start(bf16[640,320]{0,1:T(8,128)(2,1)} %param.20) | copy-start | bytes 1228804
  7.2 105.6 %all-gather.4.cloned.1.call-start = ((), (), s32[]{:S(2)}) async-start(), calls=%async_computation.2 | async-start | bytes 1638400 | tf_op jit(solution)/shard_map/all_gather | solution.py:86
  7.9 125.0 %reduce-scatter.7.cloned.1.call-start = ((), (), s32[]{:S(2)}) async-start(), calls=%async_computation.4 | async-start | bytes 819200
  73.8 40.7 %copy-start.1 = (bf16[3,1280,320]{1,2,0:T(8,128)(2,1)S(1)}, bf16[3,1280,320]{1,2,0:T(8,128)(2,1)}, u32[]{:S(2)}) copy-start(bf16[3,1280,320]{1,2,0:T(8,128)(2,1)} %param.14) | copy-start | bytes 7372804
  73.8 40.7 %copy-start.8 = (f32[1280]{0:T(1024)S(1)}, f32[1280]{0:T(1024)}, u32[]{:S(2)}) copy-start(f32[1280]{0:T(1024)} %param.13) | copy-start | bytes 15364
  111.0 58.6 %reduce-scatter.5.cloned.1.call-start = ((), (), s32[]{:S(2)}) async-start(), calls=%async_computation.3 | async-start | bytes 3276800 | tf_op jit(solution)/shard_map/reduce_scatter | solution.py:156
  114.5 2.2 %copy-start.6 = (bf16[384,320]{0,1:T(8,128)(2,1)S(1)}, bf16[384,320]{0,1:T(8,128)(2,1)}, u32[]{:S(2)}) copy-start(bf16[384,320]{0,1:T(8,128)(2,1)} %param.17) | copy-start | bytes 737284
  114.5 3.0 %copy-start.2 = (bf16[512,1280]{0,1:T(8,128)(2,1)S(1)}, bf16[512,1280]{0,1:T(8,128)(2,1)}, u32[]{:S(2)}) copy-start(bf16[512,1280]{0,1:T(8,128)(2,1)} %all-gather.4.cloned.1.call-done) | copy-start | bytes 3932164
  116.6 1.6 copy-start.7
  120.5 6.7 %copy-start.3 = (bf16[896,320]{0,1:T(8,128)(2,1)S(1)}, bf16[896,320]{0,1:T(8,128)(2,1)}, u32[]{:S(2)}) copy-start(bf16[896,320]{0,1:T(8,128)(2,1)} %pad_maximum_fusion) | copy-start | bytes 1720324
Sparse Core Ops, SparseCore 0:
  9.6 20.8 all-gather.3
  111.1 21.1 reduce-scatter.6
  134.8 34.6 reduce-scatter.4
where the time goes:
time: 179 us; the launch traced here: 178 us
  blocking collectives  92.3 us (52%)
  waiting for transfers between devices  35.7 us (20%)
  matrix products  23 us (13%)
  between operations  14.6 us (8%)
  other arithmetic  8.63 us (5%)
  local copies, waits for them, and re-layouts  3.58 us (2%)
    reduce_scatter x1, waiting for transfers between devices, body(): lax.psum_scatter(terms_pre, 'tp', scatter_dimension=1, tiled=True)  35 us
    psum x1, blocking collectives, body(): totals_all, partial_all = lax.psum((totals, partial_value), 'req')  33.5 us
    all_gather x1, blocking collectives, body(): all_queries = lax.all_gather(query_dec, 'req', axis=0, tiled=True)  31.1 us
    pmax x1, blocking collectives, body(): row_top = lax.pmax(local_top, 'req')  21.3 us
    dot_general x5, matrix products, project(): jnp.dot(hidden, w_qkv[matrix_index], preferred_element_type=jnp.float32)  7.04 us
    sub x1, matrix products, prefill_attention(): weights = jnp.where(allowed[None], jnp.exp(scores - row_top), 0.0)  6.74 us
    all_gather x1, blocking collectives, body(): lax.all_gather(x_dec, 'tp', axis=1, tiled=True)  6.32 us
  transfers between devices with their start and end apart: 3, of which 1 were waited for; matrix products, arithmetic and copies ran while one was open for 19% of the time, Pallas kernels for 0%

commit v1 on v0

v1 whole, which is shorter than its diff:
```python
import functools
import math

import jax
import jax.numpy as jnp
from jax import lax
from jax.experimental import pallas as pl
from jax.experimental.pallas import tpu as pltpu
from jax.sharding import PartitionSpec as P

HD = 80
EPSILON = 1e-06
MASKED = -1e30
CHUNK = 128
DEC_ROWS = 8
EXP_SCALE = math.log2(math.e) / math.sqrt(HD)
WINDOWS = ((0, 128), (0, 256), (128, 256), (128, 320))
F32, BF16 = jnp.float32, jnp.bfloat16


def lanes(shape, start=0):
    return lax.broadcasted_iota(jnp.int32, shape, len(shape) - 1) + start


def head_lanes(block, head):
    low, high = WINDOWS[head]
    part = block[:, low:high]
    lane = lanes(part.shape, low)
    return jnp.where((lane >= head * HD) & (lane < (head + 1) * HD), part, 0.0)


def join_heads(parts):
    lane = lanes((parts[0].shape[0], 128))
    first = jnp.where(lane < HD, parts[0], parts[1][:, :128])
    second = jnp.where(
        lane < 2 * HD - 128, parts[1][:, 128:], jnp.where(lane < 3 * HD - 128, parts[2], parts[3][:, :128])
    )
    return jnp.concatenate([first, second, parts[3][:, 128:]], axis=1)


def spread(columns, shape):
    lane = lanes(shape)
    out = jnp.broadcast_to(columns[3], shape)
    for head in (2, 1, 0):
        out = jnp.where(lane < (head + 1) * HD, columns[head], out)
    return out


def dot(a, b):
    return jnp.dot(a, b, preferred_element_type=F32)


def dot_nt(a, b):
    return lax.dot_general(a, b, (((1,), (1,)), ((), ())), preferred_element_type=F32)


def each(count, step):
    if count <= 16:
        for k in range(1, count):
            step(k)
    else:

        def loop(k, carry):
            step(k)
            return carry

        lax.fori_loop(1, count, loop, 0)


def kernel(
    n,
    x_pre,
    x_dec,
    gain,
    w_qkv,
    w_out,
    pre_keys,
    pre_values,
    pre_lens,
    dec_keys,
    dec_values,
    dec_lens,
    out_pre,
    out_dec,
    xg,
    xdg,
    wq,
    wo,
    wsel,
    kall,
    vall,
    dk,
    dv,
    qg,
    part,
    pr,
    att,
    attd,
    own,
    psend,
    precv,
    ownd,
    pdsend,
    pdrecv,
    load_sem,
    xy_sem,
    xc_sem,
    xf_sem,
    wo_sem,
    q_sem,
    p_sem,
    a_sem,
    o_sem,
):
    rows = x_pre.shape[0]
    cached = pre_keys.shape[0]
    pool = dec_keys.shape[0]
    width = x_pre.shape[1]
    own_rows = x_dec.shape[0]
    chunks = rows // CHUNK
    me = lax.axis_index("req")
    t = lax.axis_index("tp")
    core = lax.rem(t, 2)
    half = lax.div(t, 2)
    mate = t + 1 - 2 * core
    across = lax.rem(t + 2, 4)

    def remote(src, dst, sems, at, where):
        return pltpu.make_async_remote_copy(
            src_ref=src,
            dst_ref=dst,
            send_sem=sems.at[0, at],
            recv_sem=sems.at[1, at],
            device_id=where,
            device_id_type=pl.DeviceIdType.MESH,
        )

    def chunk(i):
        return pl.ds(i * CHUNK, CHUNK)

    load_x = pltpu.make_async_copy(x_pre, xg.at[t], load_sem.at[0])
    load_wq = pltpu.make_async_copy(w_qkv, wq, load_sem.at[1])
    load_pk = pltpu.make_async_copy(pre_keys, kall.at[pl.ds(0, cached)], load_sem.at[2])
    load_pv = pltpu.make_async_copy(pre_values, vall.at[pl.ds(0, cached)], load_sem.at[3])
    load_dk = pltpu.make_async_copy(dec_keys, dk, load_sem.at[4])
    load_dv = pltpu.make_async_copy(dec_values, dv, load_sem.at[5])
    load_wo = pltpu.make_async_copy(w_out, wo.at[core], load_sem.at[6])
    load_x.start()
    load_wq.start()
    load_pk.start()
    load_pv.start()

    barrier = pltpu.get_barrier_semaphore()
    for peer in (mate, across):
        pl.semaphore_signal(barrier, inc=1, device_id={"tp": peer}, device_id_type=pl.DeviceIdType.MESH)

    def greet(k):
        pl.semaphore_signal(
            barrier, inc=1, device_id={"req": lax.rem(me + k, n)}, device_id_type=pl.DeviceIdType.MESH
        )

    each(n, greet)
    dec_own = x_dec[...].astype(F32)
    xdg[t] = jnp.zeros((DEC_ROWS, width), F32)
    xdg[t, 0:own_rows] = dec_own
    pl.semaphore_wait(barrier, n + 1)

    def x_copies(sems, where, owner):
        copies = [remote(xdg.at[owner], xdg.at[owner], sems, chunks, where)]
        for i in range(chunks):
            src = x_pre.at[chunk(i)] if owner is t else xg.at[owner, chunk(i)]
            copies.append(remote(src, xg.at[owner, chunk(i)], sems, i, where))
        return copies

    over = x_copies(xy_sem, {"tp": across}, t)
    beside = x_copies(xc_sem, {"tp": mate}, t)
    passed = x_copies(xf_sem, {"tp": mate}, across)
    for i in range(chunks + 1):
        over[i].start()
    for i in range(chunks + 1):
        beside[i].start()
    load_wo.start()
    load_dk.start()
    load_dv.start()
    share_wo = remote(w_out, wo.at[core], wo_sem, 0, {"tp": mate})
    share_wo.start()

    def pass_on(i):
        over[i].wait_recv()
        passed[i].start()

    gain_row = gain[...]

    def normalize(pieces):
        tokens = jnp.concatenate(pieces, axis=1)
        mean_square = jnp.sum(tokens * tokens, axis=-1, keepdims=True) * (1.0 / tokens.shape[1])
        return tokens * lax.rsqrt(mean_square + EPSILON) * gain_row

    pass_on(0)
    pass_on(1)
    beside[0].wait_recv()
    passed[0].wait_recv()
    dec_normed = normalize([xdg[p] for p in range(4)])
    load_x.wait()

    prefix = pre_lens[0]
    prefix_bias = jnp.where(lanes((1, cached)) < prefix, 0.0, MASKED)
    tri = (CHUNK, CHUNK)
    causal_bias = jnp.where(lanes(tri) <= lax.broadcasted_iota(jnp.int32, tri, 0), 0.0, MASKED)

    def project(i):
        beside[i + 1].wait_recv()
        passed[i + 1].wait_recv()
        normed = normalize([xg[p, chunk(i)].astype(F32) for p in range(4)]).astype(BF16)
        if i == 0:
            extra = jnp.concatenate([dec_normed, dec_normed], axis=0).astype(BF16)
            normed = jnp.concatenate([normed, extra], axis=0)
            load_wq.wait()
        return [dot(normed, wq[m]).astype(BF16) for m in range(3)]

    def attend(i, query):
        seen = cached + (i + 1) * CHUNK
        parts = []
        for head in range(4):
            low, high = WINDOWS[head]
            q = head_lanes(query, head)
            scores = dot_nt(q, kall[0:seen, low:high])
            pieces = [scores[:, :cached] + prefix_bias]
            if i > 0:
                pieces.append(scores[:, cached : seen - CHUNK])
            pieces.append(scores[:, seen - CHUNK :] + causal_bias)
            scores = jnp.concatenate(pieces, axis=1)
            top = jnp.max(scores, axis=-1, keepdims=True)
            weights = jnp.exp2((scores - top) * EXP_SCALE)
            total = jnp.sum(weights, axis=-1, keepdims=True)
            parts.append(dot(weights.astype(BF16), vall[0:seen, low:high]) / total)
        att[core, chunk(i)] = join_heads(parts).astype(BF16)

    att_copies = [
        remote(att.at[core, chunk(i)], att.at[core, chunk(i)], a_sem, i, {"tp": mate}) for i in range(chunks)
    ]
    attd_copy = remote(attd.at[core], attd.at[core], a_sem, chunks, {"tp": mate})
    out_copies = [remote(psend.at[chunk(i)], precv.at[chunk(i)], o_sem, i, {"tp": across}) for i in range(chunks)]
    outd_copy = remote(pdsend, pdrecv, o_sem, chunks, {"tp": across})

    def out_terms(a, to):
        return dot(a[0], wsel[to, 0]) + dot(a[1], wsel[to, 1])

    def out_project(i, with_dec):
        att_copies[i].wait_recv()
        a = [att[c, chunk(i)] for c in range(2)]
        if with_dec:
            attd_copy.wait_recv()
            d = [attd[c] for c in range(2)]
            a = [
                jnp.concatenate([a[c], jnp.concatenate([d[c], d[c]], axis=0).astype(BF16)], axis=0)
                for c in range(2)
            ]
        sent = out_terms(a, 1 - half)
        psend[chunk(i)] = sent[:CHUNK].astype(BF16)
        out_copies[i].start()
        if with_dec:
            pdsend[...] = sent[CHUNK : CHUNK + DEC_ROWS]
            outd_copy.start()
        kept = out_terms(a, half)
        own[chunk(i)] = kept[:CHUNK]
        if with_dec:
            ownd[...] = kept[CHUNK : CHUNK + DEC_ROWS]

    def finish(i):
        out_copies[i].wait_recv()
        out_pre[chunk(i)] = (own[chunk(i)] + precv[chunk(i)].astype(F32)).astype(BF16)

    def q_copy(k):
        return remote(qg.at[me], qg.at[me], q_sem, k, {"req": lax.rem(me + k, n)})

    def p_copy(k):
        to = lax.rem(me + k, n)
        return remote(part.at[to], pr.at[me], p_sem, k, {"req": to})

    def decode_partials():
        each(n, lambda k: q_copy(k).wait_recv())
        load_dk.wait()
        load_dv.wait()
        queries = qg[...].reshape(n * DEC_ROWS, width).astype(BF16)
        lens = dec_lens[...].astype(F32)
        grid = (n * DEC_ROWS, lens.shape[1])
        row = lax.broadcasted_iota(jnp.int32, grid, 0)
        place = lax.rem(row, DEC_ROWS)
        request = lax.div(row, DEC_ROWS) * own_rows + place
        real = place < own_rows
        column = lanes(grid)
        start = jnp.sum(jnp.where(real & (column < request), lens, 0.0), axis=-1, keepdims=True)
        end = jnp.sum(jnp.where(real & (column <= request), lens, 0.0), axis=-1, keepdims=True)
        pool_row = (me * pool + lanes((1, pool))).astype(F32)
        allowed = (pool_row >= start) & (pool_row < end)
        parts = []
        stats = jnp.zeros((n * DEC_ROWS, 128), F32)
        stat_lane = lanes(stats.shape)
        for head in range(4):
            low, high = WINDOWS[head]
            scores = dot_nt(head_lanes(queries, head), dk[:, low:high])
            scores = jnp.where(allowed, scores, MASKED)
            top = jnp.max(scores, axis=-1, keepdims=True)
            weights = jnp.where(allowed, jnp.exp2((scores - top) * EXP_SCALE), 0.0)
            total = jnp.sum(weights, axis=-1, keepdims=True)
            parts.append(dot(weights.astype(BF16), dv[:, low:high]))
            stats = jnp.where(stat_lane == head, top, jnp.where(stat_lane == 4 + head, total, stats))
        part[:, :, 0:width] = join_heads(parts).reshape(n, DEC_ROWS, width)
        part[:, :, 384:512] = stats.reshape(n, DEC_ROWS, 128)
        each(n, lambda k: p_copy(k).start())
        pr[me] = part[me]

    def decode_combine(q, k, v):
        each(n, lambda j: p_copy(j).wait_recv())
        sums = pr[:, :, 0:width]
        stats = pr[:, :, 384:512]
        tops, totals, selves, factors = [], [], [], []
        product = q * k
        lane = lanes(product.shape)
        for head in range(4):
            inside = (lane >= head * HD) & (lane < (head + 1) * HD)
            self_score = jnp.sum(jnp.where(inside, product, 0.0), axis=-1, keepdims=True)
            local = stats[:, :, head : head + 1]
            top = jnp.maximum(jnp.max(local, axis=0), self_score)
            factor = jnp.exp2((local - top[None]) * EXP_SCALE)
            self_weight = jnp.exp2((self_score - top) * EXP_SCALE)
            totals.append(jnp.sum(factor * stats[:, :, 4 + head : 5 + head], axis=0) + self_weight)
            selves.append(self_weight.astype(BF16).astype(F32))
            factors.append(factor)
        mixed = jnp.sum(spread(factors, sums.shape) * sums, axis=0)
        mixed = mixed + spread(selves, v.shape) * v
        attd[core] = (mixed / spread(totals, v.shape)).astype(BF16).astype(F32)
        attd_copy.start()

    for i in range(chunks):
        q, k, v = project(i)
        at = pl.ds(cached + i * CHUNK, CHUNK)
        kall[at] = k[:CHUNK]
        vall[at] = v[:CHUNK]
        if i == 0:
            q_own, k_own, v_own = (a[CHUNK:].astype(F32)[:DEC_ROWS] for a in (q, k, v))
            qg[me] = q_own
            each(n, lambda j: q_copy(j).start())
            load_pk.wait()
            load_pv.wait()
        if i + 1 < chunks:
            pass_on(i + 2)
        attend(i, q[:CHUNK])
        att_copies[i].start()
        if i == 0:
            load_wo.wait()
            share_wo.wait_recv()
            for c in range(2):

                @pl.when(core == c)
                def _():
                    for to in range(2):
                        first = (2 * to + c) * width
                        for r in range(2):
                            wsel[to, r] = wo[r, :, first : first + width]

            decode_partials()
        if i == chunks - 2:
            decode_combine(q_own, k_own, v_own)
        if i > 0:
            out_project(i - 1, False)
    out_project(chunks - 1, True)
    for i in range(chunks):
        finish(i)
    outd_copy.wait_recv()
    out_dec[...] = (ownd[...] + pdrecv[...])[:own_rows].astype(BF16)

    for copy in over + beside + passed + [share_wo] + att_copies + [attd_copy] + out_copies + [outd_copy]:
        copy.wait_send()
    each(n, lambda k: q_copy(k).wait_send())
    each(n, lambda k: p_copy(k).wait_send())


def body(n, x_pre, x_dec, norm_gain, w_qkv, w_out, pre_keys, pre_values, pre_lens, dec_keys, dec_values, dec_lens):
    rows, width = x_pre.shape
    cached, pool = pre_keys.shape[0], dec_keys.shape[0]
    chunks = rows // CHUNK
    hbm = pl.BlockSpec(memory_space=pl.ANY)
    vmem = pl.BlockSpec(memory_space=pltpu.VMEM)
    smem = pl.BlockSpec(memory_space=pltpu.SMEM)
    dma = pltpu.SemaphoreType.DMA
    return pl.pallas_call(
        functools.partial(kernel, n),
        out_shape=(jax.ShapeDtypeStruct(x_pre.shape, BF16), jax.ShapeDtypeStruct(x_dec.shape, BF16)),
        in_specs=[hbm, vmem, vmem, hbm, hbm, hbm, hbm, smem, hbm, hbm, vmem],
        out_specs=(vmem, vmem),
        scratch_shapes=[
            pltpu.VMEM((4, rows, width), BF16),
            pltpu.VMEM((4, DEC_ROWS, width), F32),
            pltpu.VMEM(w_qkv.shape, BF16),
            pltpu.VMEM((2,) + w_out.shape, BF16),
            pltpu.VMEM((2, 2, width, width), BF16),
            pltpu.VMEM((cached + rows, width), BF16),
            pltpu.VMEM((cached + rows, width), BF16),
            pltpu.VMEM((pool, width), BF16),
            pltpu.VMEM((pool, width), BF16),
            pltpu.VMEM((n, DEC_ROWS, width), F32),
            pltpu.VMEM((n, DEC_ROWS, 512), F32),
            pltpu.VMEM((n, DEC_ROWS, 512), F32),
            pltpu.VMEM((2, rows, width), BF16),
            pltpu.VMEM((2, DEC_ROWS, width), F32),
            pltpu.VMEM((rows, width), F32),
            pltpu.VMEM((rows, width), BF16),
            pltpu.VMEM((rows, width), BF16),
            pltpu.VMEM((DEC_ROWS, width), F32),
            pltpu.VMEM((DEC_ROWS, width), F32),
            pltpu.VMEM((DEC_ROWS, width), F32),
            dma((7,)),
            dma((2, chunks + 1)),
            dma((2, chunks + 1)),
            dma((2, chunks + 1)),
            dma((2, 1)),
            dma((2, n)),
            dma((2, n)),
            dma((2, chunks + 1)),
            dma((2, chunks + 1)),
        ],
        compiler_params=pltpu.CompilerParams(
            collective_id=0, has_side_effects=True, vmem_limit_bytes=48 * 1024 * 1024
        ),
        cost_estimate=pl.CostEstimate(flops=4_000_000_000, bytes_accessed=6_000_000, transcendentals=2_000_000),
    )(
        x_pre,
        x_dec,
        norm_gain.reshape(1, -1),
        w_qkv,
        w_out,
        pre_keys,
        pre_values,
        pre_lens,
        dec_keys,
        dec_values,
        dec_lens.reshape(1, -1),
    )


def solution(mesh):
    return jax.shard_map(
        functools.partial(body, mesh.shape["req"]),
        mesh=mesh,
        in_specs=(
            P("req", "tp"),
            P("req", "tp"),
            P(),
            P(None, None, "tp"),
            P("tp", None),
            P("req", "tp"),
            P("req", "tp"),
            P("req"),
            P("req", "tp"),
            P("req", "tp"),
            P(),
        ),
        out_specs=(P("req", "tp"), P("req", "tp")),
        check_vma=False,
    )
```

time: 179 us -> 56.9 us (0.32)
  blocking collectives: 92.3 us -> 0 us
  waiting for transfers between devices: 35.7 us -> 0 us
  Pallas kernels: 0 us -> 34 us
  matrix products: 23 us -> 0 us
  local copies, waits for them, and re-layouts: 3.58 us -> 20.9 us
  between operations: 14.6 us -> 1.42 us
  other arithmetic: 8.63 us -> 0 us
    all_gather x2 -> x0, blocking collectives: 37.5 us -> none  [the longest x1 31.1 us: body(): all_queries = lax.all_gather(query_dec, 'req', axis=0, tiled=True)]
    reduce_scatter x1 -> x0, waiting for transfers between devices: 35 us -> none  [body(): lax.psum_scatter(terms_pre, 'tp', scatter_dimension=1, tiled=True)]
    pallas_call x0 -> x1, Pallas kernels: none -> 34 us  [body(): pl.pallas_call(functools.partial(kernel, n), out_shape=(jax.ShapeDtypeStr...]
    psum x1 -> x0, blocking collectives: 33.5 us -> none  [body(): totals_all, partial_all = lax.psum((totals, partial_value), 'req')]
    pmax x1 -> x0, blocking collectives: 21.3 us -> none  [body(): row_top = lax.pmax(local_top, 'req')]
    unnamed x19 -> x25, local copies, waits for them, and re-layouts: 1.66 us -> 18.3 us
    dot_general x9 -> x0, matrix products: 13.3 us -> none  [the longest x5 7.04 us: project(): jnp.dot(hidden, w_qkv[matrix_index], preferred_element_type=jnp.float32)]
    sub x1 -> x0, matrix products: 6.74 us -> none  [prefill_attention(): weights = jnp.where(allowed[None], jnp.exp(scores - row_top), 0.0)]
  transfers between devices with their start and end apart: 3 -> 0, of which waited for: 1 -> 0; matrix products, arithmetic and copies ran while one was open for 19% -> 0% of each run, Pallas kernels for 0% -> 0%
where the time goes in v1:
time: 56.9 us; the launch traced here: 56.3 us
  Pallas kernels  34 us (60%)
  local copies, waits for them, and re-layouts  20.9 us (37%)
  between operations  1.42 us (2%)
    pallas_call x1, Pallas kernels, body(): pl.pallas_call(functools.partial(kernel, n), out_shape=(jax.ShapeDtypeStr...  34 us
    unnamed x25, local copies, waits for them, and re-layouts  18.3 us
    pallas_call x1, local copies, waits for them, and re-layouts, body(): pl.pallas_call(functools.partial(kernel, n), out_shape=(jax.ShapeDtypeStr...  1.88 us

profile of v1, /device:TPU:0, one launch (start us, length us, event | category | flops | bytes accessed | tf_op | source)
XLA Modules:
  0.0 56.3 jit_solution(18400999315117565261)
XLA Ops:
  0.6 0.0 copy-start.8
  1.3 0.7 %reshape.10.gain = f32[1,1280]{1,0:T(1,128)S(1)} reshape(f32[1280]{0:T(1024)} %param.13) | data formatting | bytes 10240 | tf_op jit(solution)/shard_map/reshape | solution.py:431
  2.0 1.8 %copy.15.pre_keys = bf16[384,320]{1,0:T(8,128)(2,1)} copy(bf16[384,320]{0,1:T(8,128)(2,1)} %param.16) | data formatting | bytes 491520 | tf_op args[5]
  3.9 1.9 %copy.16.pre_values = bf16[384,320]{1,0:T(8,128)(2,1)} copy(bf16[384,320]{0,1:T(8,128)(2,1)} %param.17) | data formatting | bytes 491520 | tf_op args[6]
  5.7 1.9 %copy.13.x_pre = bf16[512,320]{1,0:T(8,128)(2,1)} copy(bf16[512,320]{0,1:T(8,128)(2,1)} %param.11) | data formatting | bytes 655360 | tf_op args[0]
  7.6 1.3 %copy.17.dec_keys = bf16[640,320]{1,0:T(8,128)(2,1)S(1)} copy(bf16[640,320]{0,1:T(8,128)(2,1)} %param.19) | data formatting | bytes 819200 | tf_op args[8]
  8.9 0.0 copy-done.8
  8.9 0.0 copy-start.6
  8.9 0.0 copy-start.7
  8.9 1.0 %copy.18.dec_values = bf16[640,320]{1,0:T(8,128)(2,1)} copy(bf16[640,320]{0,1:T(8,128)(2,1)S(1)} %copy-done.8) | data formatting | bytes 819200 | tf_op args[9]
  9.9 4.0 %copy.14.w_qkv = bf16[3,1280,320]{2,1,0:T(8,128)(2,1)S(1)} copy(bf16[3,1280,320]{1,2,0:T(8,128)(2,1)} %param.14) | data formatting | bytes 4915200 | tf_op args[3]
  14.0 0.0 copy-done.6
  14.0 0.0 copy-done.7
  14.0 0.0 copy-start
  14.0 1.0 %copy-done = bf16[640,320]{1,0:T(8,128)(2,1)S(1)} copy-done((bf16[640,320]{1,0:T(8,128)(2,1)S(1)}, bf16[640,320]{1,0:T(8,128)(2,1)}, u32[]{:S(2)}) %copy-start) | copy-done | bytes 409624
  15.0 0.0 copy-start.2
  15.0 1.0 %copy-done.2 = bf16[512,320]{1,0:T(8,128)(2,1)S(1)} copy-done((bf16[512,320]{1,0:T(8,128)(2,1)S(1)}, bf16[512,320]{1,0:T(8,128)(2,1)}, u32[]{:S(2)}) %copy-start.2) | copy-done | bytes 327704
  16.0 0.0 copy-start.3
  16.0 1.0 %copy-done.3 = bf16[384,320]{1,0:T(8,128)(2,1)S(1)} copy-done((bf16[384,320]{1,0:T(8,128)(2,1)S(1)}, bf16[384,320]{1,0:T(8,128)(2,1)}, u32[]{:S(2)}) %copy-start.3) | copy-done | bytes 245784
  17.0 0.0 copy-start.4
  17.0 1.0 %copy-done.4 = bf16[384,320]{1,0:T(8,128)(2,1)S(1)} copy-done((bf16[384,320]{1,0:T(8,128)(2,1)S(1)}, bf16[384,320]{1,0:T(8,128)(2,1)}, u32[]{:S(2)}) %copy-start.4) | copy-done | bytes 245784
  17.9 0.0 copy-start.5
  17.9 1.1 %copy-done.5 = bf16[320,1280]{1,0:T(8,128)(2,1)S(1)} copy-done((bf16[320,1280]{1,0:T(8,128)(2,1)S(1)}, bf16[320,1280]{1,0:T(8,128)(2,1)}, u32[]{:S(2)}) %copy-start.5) | copy-done | bytes 819224
  19.1 34.0 %shard_map.122 = (bf16[512,320]{1,0:T(8,128)(2,1)S(1)}, bf16[4,320]{1,0:T(4,128)(2,1)S(1)}) custom-call(bf16[512,320]{1,0:T(8,128)(2,1)S(1)} %copy-done.2, bf16[4,320]{1,0:T(4,128)(2,1)S(1)} %copy-done.6, f32[1,1280]{1,0:T(1,128)S(1)} %reshape.10.gain, bf16[3,1280,320]{2,1,0:T(8,128)(2,1)S(1)} %copy.14.w_qkv, bf16[320,1280]{1,0:T(8,128)(2,1)S(1)} %copy-done.5, ...), custom_call_target="tpu_custom_call" | custom-call | flops 4000000000 | bytes 6000000 | tf_op jit(solution)/shard_map/pallas_call | solution.py:388
  53.1 0.0 copy-start.1
  53.1 0.7 %copy-done.1 = bf16[512,320]{1,0:T(8,128)(2,1)} copy-done((bf16[512,320]{1,0:T(8,128)(2,1)}, bf16[512,320]{1,0:T(8,128)(2,1)S(1)}, u32[]{:S(2)}) %copy-start.1) | copy-done | bytes 327704
  53.8 1.9 %copy.19 = bf16[512,320]{0,1:T(8,128)(2,1)} copy(bf16[512,320]{1,0:T(8,128)(2,1)} %copy-done.1) | data formatting | bytes 655360 | tf_op jit(solution)/shard_map/pallas_call | solution.py:388
  55.7 0.6 %copy.22 = bf16[4,320]{1,0:T(4,128)(2,1)} copy(bf16[4,320]{1,0:T(4,128)(2,1)S(1)} %get-tuple-element.7) | data formatting | bytes 5120
Async XLA Ops:
  0.6 8.3 %copy-start.8 = (bf16[640,320]{0,1:T(8,128)(2,1)S(1)}, bf16[640,320]{0,1:T(8,128)(2,1)}, u32[]{:S(2)}) copy-start(bf16[640,320]{0,1:T(8,128)(2,1)} %param.20) | copy-start | bytes 1228804
  8.9 5.1 %copy-start.6 = (bf16[4,320]{1,0:T(4,128)(2,1)S(1)}, bf16[4,320]{1,0:T(4,128)(2,1)}, u32[]{:S(2)}) copy-start(bf16[4,320]{1,0:T(4,128)(2,1)} %x_dec.1) | copy-start | bytes 7684
  8.9 5.1 %copy-start.7 = (s32[32]{0:T(128)S(1)}, s32[32]{0:T(128)}, u32[]{:S(2)}) copy-start(s32[32]{0:T(128)} %param.21) | copy-start | bytes 388
  14.0 1.0 %copy-start = (bf16[640,320]{1,0:T(8,128)(2,1)S(1)}, bf16[640,320]{1,0:T(8,128)(2,1)}, u32[]{:S(2)}) copy-start(bf16[640,320]{1,0:T(8,128)(2,1)} %copy.18.dec_values) | copy-start | bytes 1228804
  15.0 1.0 %copy-start.2 = (bf16[512,320]{1,0:T(8,128)(2,1)S(1)}, bf16[512,320]{1,0:T(8,128)(2,1)}, u32[]{:S(2)}) copy-start(bf16[512,320]{1,0:T(8,128)(2,1)} %copy.13.x_pre) | copy-start | bytes 983044
  16.0 1.0 %copy-start.3 = (bf16[384,320]{1,0:T(8,128)(2,1)S(1)}, bf16[384,320]{1,0:T(8,128)(2,1)}, u32[]{:S(2)}) copy-start(bf16[384,320]{1,0:T(8,128)(2,1)} %copy.15.pre_keys) | copy-start | bytes 737284
  17.0 1.0 %copy-start.4 = (bf16[384,320]{1,0:T(8,128)(2,1)S(1)}, bf16[384,320]{1,0:T(8,128)(2,1)}, u32[]{:S(2)}) copy-start(bf16[384,320]{1,0:T(8,128)(2,1)} %copy.16.pre_values) | copy-start | bytes 737284
  17.9 1.1 %copy-start.5 = (bf16[320,1280]{1,0:T(8,128)(2,1)S(1)}, bf16[320,1280]{1,0:T(8,128)(2,1)}, u32[]{:S(2)}) copy-start(bf16[320,1280]{1,0:T(8,128)(2,1)} %w_out.1) | copy-start | bytes 2457604
  53.1 0.7 %copy-start.1 = (bf16[512,320]{1,0:T(8,128)(2,1)}, bf16[512,320]{1,0:T(8,128)(2,1)S(1)}, u32[]{:S(2)}) copy-start(bf16[512,320]{1,0:T(8,128)(2,1)S(1)} %get-tuple-element.2) | copy-start | bytes 983044

commit v2 on v1

--- a/solution.py
+++ b/solution.py
@@ -84,6 +84,7 @@
     out_dec,
     xg,
     xdg,
+    gain_t,
     wq,
     wo,
     wsel,
@@ -112,10 +113,9 @@
     a_sem,
     o_sem,
 ):
-    rows = x_pre.shape[0]
-    cached = pre_keys.shape[0]
-    pool = dec_keys.shape[0]
-    width = x_pre.shape[1]
+    width, rows = x_pre.shape
+    cached = pre_keys.shape[1]
+    pool = dec_keys.shape[1]
     own_rows = x_dec.shape[0]
     chunks = rows // CHUNK
     me = lax.axis_index("req")
@@ -138,14 +138,17 @@
     def chunk(i):
         return pl.ds(i * CHUNK, CHUNK)
 
-    load_x = pltpu.make_async_copy(x_pre, xg.at[t], load_sem.at[0])
+    load_x = [
+        pltpu.make_async_copy(x_pre.at[:, chunk(i)], xg.at[t, i], load_sem.at[6 + i]) for i in range(chunks)
+    ]
     load_wq = pltpu.make_async_copy(w_qkv, wq, load_sem.at[1])
-    load_pk = pltpu.make_async_copy(pre_keys, kall.at[pl.ds(0, cached)], load_sem.at[2])
-    load_pv = pltpu.make_async_copy(pre_values, vall.at[pl.ds(0, cached)], load_sem.at[3])
+    load_pk = pltpu.make_async_copy(pre_keys, kall.at[:, pl.ds(0, cached)], load_sem.at[2])
+    load_pv = pltpu.make_async_copy(pre_values, vall.at[:, pl.ds(0, cached)], load_sem.at[3])
     load_dk = pltpu.make_async_copy(dec_keys, dk, load_sem.at[4])
     load_dv = pltpu.make_async_copy(dec_values, dv, load_sem.at[5])
-    load_wo = pltpu.make_async_copy(w_out, wo.at[core], load_sem.at[6])
-    load_x.start()
+    load_wo = pltpu.make_async_copy(w_out, wo.at[core], load_sem.at[0])
+    for i in range(chunks):
+        load_x[i].start()
     load_wq.start()
     load_pk.start()
     load_pv.start()
@@ -163,13 +166,15 @@
     dec_own = x_dec[...].astype(F32)
     xdg[t] = jnp.zeros((DEC_ROWS, width), F32)
     xdg[t, 0:own_rows] = dec_own
+    gain_row = gain[...]
+    gain_t[...] = jnp.broadcast_to(gain_row, (CHUNK, gain_row.shape[1])).T
     pl.semaphore_wait(barrier, n + 1)
 
     def x_copies(sems, where, owner):
         copies = [remote(xdg.at[owner], xdg.at[owner], sems, chunks, where)]
         for i in range(chunks):
-            src = x_pre.at[chunk(i)] if owner is t else xg.at[owner, chunk(i)]
-            copies.append(remote(src, xg.at[owner, chunk(i)], sems, i, where))
+            src = x_pre.at[:, chunk(i)] if owner is t else xg.at[owner, i]
+            copies.append(remote(src, xg.at[owner, i], sems, i, where))
         return copies
 
     over = x_copies(xy_sem, {"tp": across}, t)
@@ -189,19 +194,15 @@
         over[i].wait_recv()
         passed[i].start()
 
-    gain_row = gain[...]
-
-    def normalize(pieces):
-        tokens = jnp.concatenate(pieces, axis=1)
-        mean_square = jnp.sum(tokens * tokens, axis=-1, keepdims=True) * (1.0 / tokens.shape[1])
-        return tokens * lax.rsqrt(mean_square + EPSILON) * gain_row
+    def normalize(tokens, axis, scale):
+        mean_square = jnp.sum(tokens * tokens, axis=axis, keepdims=True) * (1.0 / tokens.shape[axis])
+        return tokens * lax.rsqrt(mean_square + EPSILON) * scale
 
     pass_on(0)
     pass_on(1)
     beside[0].wait_recv()
     passed[0].wait_recv()
-    dec_normed = normalize([xdg[p] for p in range(4)])
-    load_x.wait()
+    dec_normed = normalize(jnp.concatenate([xdg[p] for p in range(4)], axis=1), 1, gain_row)
 
     prefix = pre_lens[0]
     prefix_bias = jnp.where(lanes((1, cached)) < prefix, 0.0, MASKED)
@@ -211,12 +212,14 @@
     def project(i):
         beside[i + 1].wait_recv()
         passed[i + 1].wait_recv()
-        normed = normalize([xg[p, chunk(i)].astype(F32) for p in range(4)]).astype(BF16)
+        load_x[i].wait()
+        tokens = jnp.concatenate([xg[p, i].astype(F32) for p in range(4)], axis=0)
+        normed = normalize(tokens, 0, gain_t[...]).astype(BF16)
         if i == 0:
-            extra = jnp.concatenate([dec_normed, dec_normed], axis=0).astype(BF16)
-            normed = jnp.concatenate([normed, extra], axis=0)
+            extra = jnp.concatenate([dec_normed] * (CHUNK // DEC_ROWS), axis=0).T.astype(BF16)
+            normed = jnp.concatenate([normed, extra], axis=1)
             load_wq.wait()
-        return [dot(normed, wq[m]).astype(BF16) for m in range(3)]
+        return [dot(wq[m], normed) for m in range(3)]
 
     def attend(i, query):
         seen = cached + (i + 1) * CHUNK
@@ -224,7 +227,7 @@
         for head in range(4):
             low, high = WINDOWS[head]
             q = head_lanes(query, head)
-            scores = dot_nt(q, kall[0:seen, low:high])
+            scores = dot(q, kall[low:high, 0:seen])
             pieces = [scores[:, :cached] + prefix_bias]
             if i > 0:
                 pieces.append(scores[:, cached : seen - CHUNK])
@@ -233,7 +236,7 @@
             top = jnp.max(scores, axis=-1, keepdims=True)
             weights = jnp.exp2((scores - top) * EXP_SCALE)
             total = jnp.sum(weights, axis=-1, keepdims=True)
-            parts.append(dot(weights.astype(BF16), vall[0:seen, low:high]) / total)
+            parts.append(dot_nt(weights.astype(BF16), vall[low:high, 0:seen]) / total)
         att[core, chunk(i)] = join_heads(parts).astype(BF16)
 
     att_copies = [
@@ -269,7 +272,7 @@
 
     def finish(i):
         out_copies[i].wait_recv()
-        out_pre[chunk(i)] = (own[chunk(i)] + precv[chunk(i)].astype(F32)).astype(BF16)
+        out_pre[:, chunk(i)] = (own[chunk(i)] + precv[chunk(i)].astype(F32)).T.astype(BF16)
 
     def q_copy(k):
         return remote(qg.at[me], qg.at[me], q_sem, k, {"req": lax.rem(me + k, n)})
@@ -299,12 +302,12 @@
         stat_lane = lanes(stats.shape)
         for head in range(4):
             low, high = WINDOWS[head]
-            scores = dot_nt(head_lanes(queries, head), dk[:, low:high])
+            scores = dot(head_lanes(queries, head), dk[low:high])
             scores = jnp.where(allowed, scores, MASKED)
             top = jnp.max(scores, axis=-1, keepdims=True)
             weights = jnp.where(allowed, jnp.exp2((scores - top) * EXP_SCALE), 0.0)
             total = jnp.sum(weights, axis=-1, keepdims=True)
-            parts.append(dot(weights.astype(BF16), dv[:, low:high]))
+            parts.append(dot_nt(weights.astype(BF16), dv[low:high]))
             stats = jnp.where(stat_lane == head, top, jnp.where(stat_lane == 4 + head, total, stats))
         part[:, :, 0:width] = join_heads(parts).reshape(n, DEC_ROWS, width)
         part[:, :, 384:512] = stats.reshape(n, DEC_ROWS, 128)
@@ -336,17 +339,17 @@
     for i in range(chunks):
         q, k, v = project(i)
         at = pl.ds(cached + i * CHUNK, CHUNK)
-        kall[at] = k[:CHUNK]
-        vall[at] = v[:CHUNK]
+        kall[:, at] = k[:, :CHUNK].astype(BF16)
+        vall[:, at] = v[:, :CHUNK].astype(BF16)
         if i == 0:
-            q_own, k_own, v_own = (a[CHUNK:].astype(F32)[:DEC_ROWS] for a in (q, k, v))
+            q_own, k_own, v_own = (a[:, CHUNK:].T[:DEC_ROWS].astype(BF16).astype(F32) for a in (q, k, v))
             qg[me] = q_own
             each(n, lambda j: q_copy(j).start())
             load_pk.wait()
             load_pv.wait()
         if i + 1 < chunks:
             pass_on(i + 2)
-        attend(i, q[:CHUNK])
+        attend(i, q[:, :CHUNK].T.astype(BF16))
         att_copies[i].start()
         if i == 0:
             load_wo.wait()
@@ -385,21 +388,22 @@
     vmem = pl.BlockSpec(memory_space=pltpu.VMEM)
     smem = pl.BlockSpec(memory_space=pltpu.SMEM)
     dma = pltpu.SemaphoreType.DMA
-    return pl.pallas_call(
+    out_pre, out_dec = pl.pallas_call(
         functools.partial(kernel, n),
-        out_shape=(jax.ShapeDtypeStruct(x_pre.shape, BF16), jax.ShapeDtypeStruct(x_dec.shape, BF16)),
+        out_shape=(jax.ShapeDtypeStruct((width, rows), BF16), jax.ShapeDtypeStruct(x_dec.shape, BF16)),
         in_specs=[hbm, vmem, vmem, hbm, hbm, hbm, hbm, smem, hbm, hbm, vmem],
         out_specs=(vmem, vmem),
         scratch_shapes=[
-            pltpu.VMEM((4, rows, width), BF16),
+            pltpu.VMEM((4, chunks, width, CHUNK), BF16),
             pltpu.VMEM((4, DEC_ROWS, width), F32),
-            pltpu.VMEM(w_qkv.shape, BF16),
+            pltpu.VMEM((norm_gain.shape[0], CHUNK), F32),
+            pltpu.VMEM((3, width, w_qkv.shape[1]), BF16),
             pltpu.VMEM((2,) + w_out.shape, BF16),
             pltpu.VMEM((2, 2, width, width), BF16),
-            pltpu.VMEM((cached + rows, width), BF16),
-            pltpu.VMEM((cached + rows, width), BF16),
-            pltpu.VMEM((pool, width), BF16),
-            pltpu.VMEM((pool, width), BF16),
+            pltpu.VMEM((width, cached + rows), BF16),
+            pltpu.VMEM((width, cached + rows), BF16),
+            pltpu.VMEM((width, pool), BF16),
+            pltpu.VMEM((width, pool), BF16),
             pltpu.VMEM((n, DEC_ROWS, width), F32),
             pltpu.VMEM((n, DEC_ROWS, 512), F32),
             pltpu.VMEM((n, DEC_ROWS, 512), F32),
@@ -411,7 +415,7 @@
             pltpu.VMEM((DEC_ROWS, width), F32),
             pltpu.VMEM((DEC_ROWS, width), F32),
             pltpu.VMEM((DEC_ROWS, width), F32),
-            dma((7,)),
+            dma((6 + chunks,)),
             dma((2, chunks + 1)),
             dma((2, chunks + 1)),
             dma((2, chunks + 1)),
@@ -422,22 +426,23 @@
             dma((2, chunks + 1)),
         ],
         compiler_params=pltpu.CompilerParams(
-            collective_id=0, has_side_effects=True, vmem_limit_bytes=48 * 1024 * 1024
+            collective_id=0, has_side_effects=True, vmem_limit_bytes=60 * 1024 * 1024
         ),
         cost_estimate=pl.CostEstimate(flops=4_000_000_000, bytes_accessed=6_000_000, transcendentals=2_000_000),
     )(
-        x_pre,
+        x_pre.T,
         x_dec,
         norm_gain.reshape(1, -1),
-        w_qkv,
+        jnp.swapaxes(w_qkv, 1, 2),
         w_out,
-        pre_keys,
-        pre_values,
+        pre_keys.T,
+        pre_values.T,
         pre_lens,
-        dec_keys,
-        dec_values,
+        dec_keys.T,
+        dec_values.T,
         dec_lens.reshape(1, -1),
     )
+    return out_pre.T, out_dec
 
 
 def solution(mesh):

time: 56.9 us -> 41 us (0.72)
  local copies, waits for them, and re-layouts: 20.9 us -> 4.27 us
  Pallas kernels: 34 us -> 35.2 us
    unnamed x25 -> x2, local copies, waits for them, and re-layouts: 18.3 us -> 2.98 us
    pallas_call x1 -> x0, local copies, waits for them, and re-layouts: 1.88 us -> none  [body(): pl.pallas_call(functools.partial(kernel, n), out_shape=(jax.ShapeDtypeStr...]
    pallas_call x1, Pallas kernels: 34 us -> 35.2 us  [body(): pl.pallas_call(functools.partial(kernel, n), out_shape=(jax.ShapeDtypeStr...]
    reshape x1, local copies, waits for them, and re-layouts: 0.7 us -> 1.29 us  [body(): norm_gain.reshape(1, -1)]
where the time goes in v2:
time: 41 us; the launch traced here: 40.7 us
  Pallas kernels  35.2 us (86%)
  local copies, waits for them, and re-layouts  4.27 us (10%)
  between operations  1.29 us (3%)
    pallas_call x1, Pallas kernels, body(): pl.pallas_call(functools.partial(kernel, n), out_shape=(jax.ShapeDtypeStr...  35.2 us
    unnamed x2, local copies, waits for them, and re-layouts  2.98 us
    reshape x1, local copies, waits for them, and re-layouts, body(): norm_gain.reshape(1, -1)  1.29 us

profile of v2, /device:TPU:0, one launch (start us, length us, event | category | flops | bytes accessed | tf_op | source)
XLA Modules:
  0.0 40.7 jit_solution(6218508855139437014)
XLA Ops:
  1.3 1.3 %reshape.10.gain = f32[1,1280]{1,0:T(1,128)} reshape(f32[1280]{0:T(1024)} %param.13) | data formatting | bytes 10240 | tf_op jit(solution)/shard_map/reshape | solution.py:435
  2.6 35.2 %shard_map.122 = (bf16[320,512]{1,0:T(8,128)(2,1)}, bf16[4,320]{1,0:T(4,128)(2,1)}) custom-call(bf16[320,512]{1,0:T(8,128)(2,1)} %bitcast.12, bf16[4,320]{1,0:T(4,128)(2,1)} %x_dec.1, f32[1,1280]{1,0:T(1,128)} %reshape.10.gain, bf16[3,320,1280]{2,1,0:T(8,128)(2,1)} %bitcast.9, bf16[320,1280]{1,0:T(8,128)(2,1)} %w_out.1, bf16[320,384]{1,0:T(8,128)(2,1)} %bitcast.13, ...), custom_call_target="tpu_custom_call" | custom-call | flops 4000000000 | bytes 6000000 | tf_op jit(solution)/shard_map/pallas_call | solution.py:391
  37.7 1.7 %copy.16 = bf16[512,320]{0,1:T(8,128)(2,1)} copy(bf16[512,320]{0,1:T(8,128)(2,1)} %bitcast.8) | data formatting | bytes 655360
  39.5 1.3 %copy.17 = bf16[4,320]{1,0:T(4,128)(2,1)} copy(bf16[4,320]{1,0:T(4,128)(2,1)} %get-tuple-element.9) | data formatting | bytes 5120

commit v3 on v2

--- a/solution.py
+++ b/solution.py
@@ -166,7 +166,7 @@
     dec_own = x_dec[...].astype(F32)
     xdg[t] = jnp.zeros((DEC_ROWS, width), F32)
     xdg[t, 0:own_rows] = dec_own
-    gain_row = gain[...]
+    gain_row = gain[...].reshape(1, gain.shape[0])
     gain_t[...] = jnp.broadcast_to(gain_row, (CHUNK, gain_row.shape[1])).T
     pl.semaphore_wait(barrier, n + 1)
 
@@ -188,7 +188,6 @@
     load_dk.start()
     load_dv.start()
     share_wo = remote(w_out, wo.at[core], wo_sem, 0, {"tp": mate})
-    share_wo.start()
 
     def pass_on(i):
         over[i].wait_recv()
@@ -349,9 +348,11 @@
             load_pv.wait()
         if i + 1 < chunks:
             pass_on(i + 2)
+        if i == 0:
+            share_wo.start()
         attend(i, q[:, :CHUNK].T.astype(BF16))
         att_copies[i].start()
-        if i == 0:
+        if i == 1:
             load_wo.wait()
             share_wo.wait_recv()
             for c in range(2):
@@ -364,7 +365,7 @@
                             wsel[to, r] = wo[r, :, first : first + width]
 
             decode_partials()
-        if i == chunks - 2:
+        if i == chunks - 1:
             decode_combine(q_own, k_own, v_own)
         if i > 0:
             out_project(i - 1, False)
@@ -432,7 +433,7 @@
     )(
         x_pre.T,
         x_dec,
-        norm_gain.reshape(1, -1),
+        norm_gain,
         jnp.swapaxes(w_qkv, 1, 2),
         w_out,
         pre_keys.T,

time: 41 us -> 38.8 us (0.946)
  local copies, waits for them, and re-layouts: 4.27 us -> 2.98 us
  Pallas kernels: 35.2 us -> 34.3 us
    reshape x1 -> x0, local copies, waits for them, and re-layouts: 1.29 us -> none  [body(): norm_gain.reshape(1, -1)]
    pallas_call x1, Pallas kernels: 35.2 us -> 34.3 us  [body(): pl.pallas_call(functools.partial(kernel, n), out_shape=(jax.ShapeDtypeStr...]
where the time goes in v3:
time: 38.8 us; the launch traced here: 38.6 us
  Pallas kernels  34.3 us (88%)
  local copies, waits for them, and re-layouts  2.98 us (8%)
  between operations  1.29 us (3%)
    pallas_call x1, Pallas kernels, body(): pl.pallas_call(functools.partial(kernel, n), out_shape=(jax.ShapeDtypeStr...  34.3 us
    unnamed x2, local copies, waits for them, and re-layouts  2.98 us

profile of v3, /device:TPU:0, one launch (start us, length us, event | category | flops | bytes accessed | tf_op | source)
XLA Modules:
  0.0 38.6 jit_solution(18386956940227870531)
XLA Ops:
  1.3 34.3 %shard_map.122 = (bf16[320,512]{1,0:T(8,128)(2,1)}, bf16[4,320]{1,0:T(4,128)(2,1)}) custom-call(bf16[320,512]{1,0:T(8,128)(2,1)} %bitcast.12, bf16[4,320]{1,0:T(4,128)(2,1)} %x_dec.1, f32[1280]{0:T(1024)} %gain.1, bf16[3,320,1280]{2,1,0:T(8,128)(2,1)} %bitcast.9, bf16[320,1280]{1,0:T(8,128)(2,1)} %w_out.1, bf16[320,384]{1,0:T(8,128)(2,1)} %bitcast.13, ...), custom_call_target="tpu_custom_call" | custom-call | flops 4000000000 | bytes 6000000 | tf_op jit(solution)/shard_map/pallas_call | solution.py:392
  35.6 1.7 %copy.16 = bf16[512,320]{0,1:T(8,128)(2,1)} copy(bf16[512,320]{0,1:T(8,128)(2,1)} %bitcast.8) | data formatting | bytes 655360
  37.3 1.3 %copy.17 = bf16[4,320]{1,0:T(4,128)(2,1)} copy(bf16[4,320]{1,0:T(4,128)(2,1)} %get-tuple-element.9) | data formatting | bytes 5120
